TPU v7x, 32 devices: a whole 2x2x4 slice. The times are simulated.
32 devices in a mesh: dp: 8 (over y, x, core), vocab: 4 (over z).
Axes of the slice: x: 2, y: 2, z: 4, core: 2. Of those that a mesh axis runs over, the one named last changes fastest.
Arguments:
- hidden: bfloat16 [64, 3584], P('dp', 'vocab'), may hold values from -8 to 8
- head_weight: bfloat16 [4, 38016, 3584], P('vocab', 'dp'), may hold values from -1 to 1
- teacher_logits: bfloat16 [4, 32, 76032], P('vocab', 'dp'), may hold values from -20 to 310
Outputs:
- hidden_grad: bfloat16 [64, 3584], P('dp', 'vocab')
- head_grad: bfloat16 [4, 38016, 3584], P('vocab', 'dp')
All inputs are finite; a program needn't handle non-finite values.
Results may differ from a plain program's by a relative error of at most 0.011.
Values may be sent and summed in bfloat16 or wider, within the bound.
No kernel may reach another device: no remote copies, remote signals or barrier semaphores. Data moves between devices by JAX's collectives and lax.ppermute only.
A program may use at most 128 MiB of HBM per device.

v0:
```python
import functools

import jax
import jax.numpy as jnp
from jax import lax
from jax.experimental import pallas as pl
from jax.experimental.pallas import tpu as pltpu
from jax.sharding import Mesh
from jax.sharding import PartitionSpec as P

GRAD_SCALE = 32.0
F32 = jnp.float32
BF16 = jnp.bfloat16
MIB = 2**20
LANES = 128
LOWEST = -1e30
LOGIT_TILE = 512
PRODUCT_TILE = 1024


def row_tile(rows, limit):
    best = rows
    for tile in range(16, limit + 1, 16):
        if rows % tile == 0:
            best = tile
    return best


def column_tile(width, limit):
    return max(c for c in range(LANES, limit + 1, LANES) if width % c == 0)


def tile_rows(step, tile, rows):
    if tile == rows:
        return slice(None)
    return pl.ds(pl.multiple_of(step * tile, tile), tile)


def params(limit):
    return pltpu.CompilerParams(vmem_limit_bytes=limit)


def whole(shape):
    return pl.BlockSpec(shape, lambda *_: (0,) * len(shape))


def in_vmem(count):
    return [pl.BlockSpec(memory_space=pltpu.VMEM)] * count


def stream(w_ref, buffer, sems, first, tile, ahead, compute, between):
    rows = w_ref.shape[0]
    if rows < first + tile:
        first = 0
    steps = (rows - first) // tile
    begin, last = slice(0, first), slice(first + steps * tile, rows)
    rest = rows - last.start

    def copy(here, sem):
        return pltpu.make_async_copy(w_ref.at[here, :], buffer.at[here, :], sem)

    def place(step):
        return pl.ds(pl.multiple_of(first + step * tile, LANES), tile)

    ahead = min(ahead, steps)
    if first:
        copy(begin, sems.at[steps + 1]).start()
    for step in range(ahead):
        copy(place(step), sems.at[step]).start()
    if rest and ahead == steps:
        copy(last, sems.at[steps]).start()
    between()
    if first:
        copy(begin, sems.at[steps + 1]).wait()
        compute(begin, steps + 1)

    def body(step, carry):
        @pl.when(step + ahead < steps)
        def _():
            copy(place(step + ahead), sems.at[step + ahead]).start()

        if rest and ahead < steps:

            @pl.when(step + ahead == steps)
            def _():
                copy(last, sems.at[steps]).start()

        copy(place(step), sems.at[step]).wait()
        compute(place(step), step)
        return carry

    if steps:
        lax.fori_loop(0, steps, body, 0)
    if rest:
        copy(last, sems.at[steps]).wait()
        compute(last, steps)
    chunks = [(k, slice(first + k * tile, first + (k + 1) * tile)) for k in range(steps)]
    return chunks + [(steps, last)] * bool(rest) + [(steps + 1, begin)] * bool(first)


def turn(column):
    size = column.shape[0]
    row = lax.broadcasted_iota(jnp.int32, (size, size), 0)
    col = lax.broadcasted_iota(jnp.int32, (size, size), 1)
    return jnp.sum(jnp.where(row == col, column, 0.0), axis=0, keepdims=True)


def turn_back(line):
    size = line.shape[1]
    row = lax.broadcasted_iota(jnp.int32, (size, size), 0)
    col = lax.broadcasted_iota(jnp.int32, (size, size), 1)
    return jnp.sum(jnp.where(row == col, line, 0.0), axis=1, keepdims=True)


def logits_kernel(own_ref, other_ref, t_stats_ref, w_ref, *refs):
    stats_ref, lt_out, out_ref, message_ref, *scratch = refs
    lt_ref, hidden, buffer, staged, t_stats, sems, lt_sems, out_sems = scratch
    keep = pltpu.make_async_copy(hidden, out_ref, out_sems.at[0])
    load = pltpu.make_async_copy(t_stats_ref, t_stats, out_sems.at[1])
    load.start()

    def assemble():
        n_v, n_pl, _, chunk = own_ref.shape
        core = lax.axis_index("co")
        staged[core] = own_ref[...].astype(F32)
        staged[1 - core] = other_ref[...].astype(F32)
        for v in range(n_v):
            groups = [staged[c, v, p] for p in range(n_pl) for c in range(2)]
            block = jnp.concatenate(groups, axis=0)
            hidden[:, v * chunk : (v + 1) * chunk] = block.astype(BF16)
        keep.start()

    def send(here, index):
        return pltpu.make_async_copy(lt_ref.at[:, here], lt_out.at[:, here], lt_sems.at[index])

    def compute(here, index):
        lt_ref[:, here] = lax.dot_general(
            hidden[...], buffer[here, :], (((1,), (1,)), ((), ())), preferred_element_type=F32
        )
        send(here, index).start()

    chunks = stream(w_ref, buffer, sems, 256, LOGIT_TILE, 3, compute, assemble)
    values = lt_ref[...]
    top = jnp.max(values, axis=1, keepdims=True)
    total = jnp.sum(jnp.exp(values - top), axis=1, keepdims=True)
    stats_ref[...] = jnp.concatenate([top, total], axis=1)
    lines = jnp.concatenate([turn(top), turn(total)], axis=0)
    load.wait()
    lanes = t_stats.shape[1]
    if lanes > lines.shape[1]:
        lines = jnp.concatenate([lines, jnp.zeros((2, lanes - lines.shape[1]), F32)], axis=1)
    message = jnp.concatenate([lines, t_stats[...], jnp.zeros((4, lanes), F32)], axis=0)
    for k in range(message_ref.shape[0]):
        message_ref[k] = message
    keep.wait()
    for index, here in chunks:
        send(here, index).wait()


def student_logits(own, other, t_stats, weight, count):
    rows, width = weight.shape
    n_v, n_pl, group, _ = own.shape
    tokens = 2 * n_pl * group
    anywhere = pl.BlockSpec(memory_space=pl.ANY)
    return pl.pallas_call(
        logits_kernel,
        in_specs=[*in_vmem(2), anywhere, anywhere],
        out_specs=[*in_vmem(1), anywhere, anywhere, *in_vmem(1)],
        out_shape=[
            jax.ShapeDtypeStruct((tokens, 2), F32),
            pltpu.HBM((tokens, rows), F32),
            pltpu.HBM((tokens, width), BF16),
            pltpu.HBM((count, 8, t_stats.shape[1]), F32),
        ],
        scratch_shapes=[
            pltpu.VMEM((tokens, rows), F32),
            pltpu.VMEM((tokens, width), BF16),
            pltpu.VMEM((rows, width), BF16),
            pltpu.VMEM((2, *own.shape), F32),
            pltpu.VMEM(t_stats.shape, F32),
            pltpu.SemaphoreType.DMA((rows // LOGIT_TILE + 2,)),
            pltpu.SemaphoreType.DMA((rows // LOGIT_TILE + 2,)),
            pltpu.SemaphoreType.DMA((2,)),
        ],
        compiler_params=params(46 * MIB),
        cost_estimate=pl.CostEstimate(
            flops=8 * rows * width * tokens, bytes_accessed=2 * rows * width, transcendentals=0
        ),
    )(own, other, pltpu.with_memory_space_constraint(t_stats, pltpu.HBM), weight)


def copies_kernel(h_ref, out_ref, buffer, sem, sems):
    load = pltpu.make_async_copy(h_ref, buffer, sem)
    load.start()
    load.wait()
    sends = [
        pltpu.make_async_copy(buffer, out_ref.at[k], sems.at[k]) for k in range(out_ref.shape[0])
    ]
    for send in sends:
        send.start()
    for send in sends:
        send.wait()


def copies(hidden, count):
    anywhere = pl.BlockSpec(memory_space=pl.ANY)
    return pl.pallas_call(
        copies_kernel,
        in_specs=[anywhere],
        out_specs=anywhere,
        out_shape=pltpu.HBM((count, *hidden.shape), BF16),
        scratch_shapes=[
            pltpu.VMEM(hidden.shape, BF16),
            pltpu.SemaphoreType.DMA,
            pltpu.SemaphoreType.DMA((count,)),
        ],
        compiler_params=params(4 * MIB),
    )(pltpu.with_memory_space_constraint(hidden, pltpu.HBM))


def split_kernel(t_ref, out_ref, stats_ref, buffer, sem):
    load = pltpu.make_async_copy(t_ref, buffer, sem)
    load.start()
    load.wait()
    total, (count, _, cols) = buffer.shape[1], out_ref.shape
    for s in range(2):
        for d in range(count // 2):
            start = (s * (count // 2) + d) * cols
            low = start // LANES * LANES
            high = min(-(-(start + cols) // LANES) * LANES, total)
            values = buffer[:, low:high].astype(F32)
            out_ref[d * 2 + s] = values[:, start - low : start - low + cols].astype(BF16)
    values = buffer[...].astype(F32)
    half, lanes = values.shape[0], stats_ref.shape[1]
    top = jnp.max(values, axis=1, keepdims=True)
    total = jnp.sum(jnp.exp(values - top), axis=1, keepdims=True)
    group = lax.axis_index("pl") * 2 + lax.axis_index("co")
    first = (group * 2 + lax.axis_index("vs")) * half
    row = lax.broadcasted_iota(jnp.int32, (half, lanes), 0)
    lane = lax.broadcasted_iota(jnp.int32, (half, lanes), 1)
    chosen = lane == first + row
    tops = jnp.max(jnp.where(chosen, top, LOWEST), axis=0, keepdims=True)
    totals = jnp.sum(jnp.where(chosen, total, 0.0), axis=0, keepdims=True)
    stats_ref[...] = jnp.concatenate([tops, totals], axis=0)


def split_teacher(piece, n_dp):
    half, total = piece.shape
    return pl.pallas_call(
        split_kernel,
        in_specs=[pl.BlockSpec(memory_space=pl.ANY)],
        out_specs=in_vmem(2),
        out_shape=[
            pltpu.HBM((2 * n_dp, half, total // (2 * n_dp)), BF16),
            pltpu.HBM((2, -(-2 * half * n_dp // LANES) * LANES), F32),
        ],
        scratch_shapes=[pltpu.VMEM(piece.shape, BF16), pltpu.SemaphoreType.DMA],
        compiler_params=params(8 * MIB),
    )(pltpu.with_memory_space_constraint(piece, pltpu.HBM))


def teacher_values(t_ref):
    return jnp.concatenate([t_ref[j].astype(F32) for j in range(t_ref.shape[0])], axis=0)


def products_kernel(t_ref, lt_in, stats_ref, w_ref, u_ref, t_stats_ref, both_ref, *refs):
    lt_ref, buffer, packed, both, sems, own_sems = refs
    load = pltpu.make_async_copy(lt_in, lt_ref, own_sems.at[0])
    keep = pltpu.make_async_copy(both, both_ref, own_sems.at[1])
    tokens = stats_ref.shape[0]
    load.start()

    def prepare():
        values = teacher_values(t_ref)
        top = jnp.max(values, axis=1, keepdims=True)
        weights = jnp.exp(values - top)
        total = jnp.sum(weights, axis=1, keepdims=True)
        t_stats_ref[...] = jnp.concatenate([top, total], axis=1)
        teach = weights * (1.0 / total)
        load.wait()
        share = jnp.exp(lt_ref[...] - stats_ref[:, 0:1]) * (1.0 / stats_ref[:, 1:2])
        both[...] = jnp.concatenate([share, teach], axis=0).T
        packed[:tokens, :] = (share - teach).astype(BF16)
        packed[tokens:, :] = teach.astype(BF16)
        keep.start()
        u_ref[...] = jnp.zeros_like(u_ref)

    def compute(here, index):
        width = u_ref.shape[1]
        block = column_tile(width, 512)
        for k in range(0, width, block):
            cols = slice(k, k + block)
            u_ref[:, cols] += jnp.dot(
                packed[:, here], buffer[here, cols], preferred_element_type=F32
            )

    stream(w_ref, buffer, sems, 512, PRODUCT_TILE, 2, compute, prepare)
    keep.wait()


def local_products(weight, teacher, lt, stats):
    rows, width = weight.shape
    tokens = lt.shape[0]
    anywhere = pl.BlockSpec(memory_space=pl.ANY)
    return pl.pallas_call(
        products_kernel,
        in_specs=[*in_vmem(1), anywhere, *in_vmem(1), anywhere],
        out_specs=[*in_vmem(2), anywhere],
        out_shape=[
            jax.ShapeDtypeStruct((2 * tokens, width), F32),
            jax.ShapeDtypeStruct((tokens, 2), F32),
            pltpu.HBM((rows, 2 * tokens), F32),
        ],
        scratch_shapes=[
            pltpu.VMEM((tokens, rows), F32),
            pltpu.VMEM((rows, width), BF16),
            pltpu.VMEM((2 * tokens, rows), BF16),
            pltpu.VMEM((rows, 2 * tokens), F32),
            pltpu.SemaphoreType.DMA((rows // PRODUCT_TILE + 2,)),
            pltpu.SemaphoreType.DMA((2,)),
        ],
        compiler_params=params(46 * MIB),
        cost_estimate=pl.CostEstimate(
            flops=8 * rows * width * tokens, bytes_accessed=2 * rows * width, transcendentals=0
        ),
    )(teacher, pltpu.with_memory_space_constraint(lt, pltpu.HBM), stats, weight)


def combine_kernel(all_ref, s_ref, t_ref, u_ref, hp_ref, mass_ref):
    tokens = s_ref.shape[0]

    def mass(k, mine_ref):
        top_all = all_ref[:, k, :tokens]
        top = jnp.max(top_all, axis=0, keepdims=True)
        total = jnp.sum(jnp.exp(top_all - top) * all_ref[:, k + 1, :tokens], axis=0, keepdims=True)
        return jnp.exp(mine_ref[:, 0:1] - turn_back(top)) * mine_ref[:, 1:2] / turn_back(total)

    student, teacher = mass(0, s_ref), mass(2, t_ref)
    mass_ref[...] = GRAD_SCALE * jnp.concatenate([turn(student), turn(teacher)], axis=1)
    scale_x = GRAD_SCALE * student
    scale_t = GRAD_SCALE * (student - teacher)
    width = hp_ref.shape[2]
    for v in range(hp_ref.shape[0]):
        cols = slice(v * width, (v + 1) * width)
        hp_ref[v] = (u_ref[:tokens, cols] * scale_x + u_ref[tokens:, cols] * scale_t).astype(BF16)


def combine(stats_all, s_stats, t_stats, products, n_v):
    tokens = s_stats.shape[0]
    width = products.shape[1] // n_v
    return pl.pallas_call(
        combine_kernel,
        in_specs=in_vmem(4),
        out_specs=in_vmem(2),
        out_shape=[
            pltpu.HBM((n_v, tokens, width), BF16),
            jax.ShapeDtypeStruct((1, 2 * tokens), F32),
        ],
        compiler_params=params(12 * MIB),
    )(stats_all, s_stats, t_stats, products)


def head_blocks(width):
    first = column_tile(width, 512)
    rest = column_tile(width - first, 1024)
    return [(0, first)] + [(k, rest) for k in range(first, width, rest)]


def head_kernel(tile, both_ref, mass_ref, hidden_ref, out_ref, both, hidden, result, sems, out_sems):
    rows = both_ref.shape[0]
    tokens, width = hidden_ref.shape
    steps = rows // tile
    load_hidden = pltpu.make_async_copy(hidden_ref, hidden, sems.at[steps])

    def load(step):
        here = tile_rows(step, tile, rows)
        return pltpu.make_async_copy(both_ref.at[here, :], both.at[here, :], sems.at[step])

    def store(step, block, start, size):
        here, cols = tile_rows(step, tile, rows), slice(start, start + size)
        return pltpu.make_async_copy(
            result.at[here, cols], out_ref.at[here, cols], out_sems.at[step, block]
        )

    load(0).start()
    load_hidden.start()
    for step in range(1, steps):
        load(step).start()
    load_hidden.wait()

    def body(step, carry):
        load(step).wait()
        here = tile_rows(step, tile, rows)
        scaled = both[here, :] * mass_ref[...]
        grad = (scaled[:, :tokens] - scaled[:, tokens:]).astype(BF16)
        for block, (start, size) in enumerate(head_blocks(width)):
            inner = column_tile(size, 256)
            for k in range(start, start + size, inner):
                result[here, k : k + inner] = jnp.dot(
                    grad, hidden[:, k : k + inner], preferred_element_type=F32
                ).astype(BF16)
            store(step, block, start, size).start()
        return carry

    lax.fori_loop(0, steps, body, 0)
    for step in range(steps):
        for block, (start, size) in enumerate(head_blocks(width)):
            store(step, block, start, size).wait()


def head_gradient(both, mass, hidden):
    rows = both.shape[0]
    tokens, width = hidden.shape
    tile = row_tile(rows, 1584)
    steps = rows // tile
    anywhere = pl.BlockSpec(memory_space=pl.ANY)
    in_hbm = lambda x: pltpu.with_memory_space_constraint(x, pltpu.HBM)
    return pl.pallas_call(
        functools.partial(head_kernel, tile),
        in_specs=[anywhere, *in_vmem(1), anywhere],
        out_specs=anywhere,
        out_shape=jax.ShapeDtypeStruct((rows, width), BF16),
        scratch_shapes=[
            pltpu.VMEM((rows, 2 * tokens), F32),
            pltpu.VMEM((tokens, width), BF16),
            pltpu.VMEM((rows, width), BF16),
            pltpu.SemaphoreType.DMA((steps + 1,)),
            pltpu.SemaphoreType.DMA((steps, len(head_blocks(width)))),
        ],
        compiler_params=params(46 * MIB),
        cost_estimate=pl.CostEstimate(
            flops=8 * rows * width * tokens, bytes_accessed=2 * rows * width, transcendentals=0
        ),
    )(in_hbm(both), mass, in_hbm(hidden))


def exchange(parts, axes):
    return lax.all_to_all(parts, axes, split_axis=0, concat_axis=0, tiled=True)


def shards(n_dp, n_v, hidden, head_weight, teacher_logits):
    everyone = ("vk", "vs", "pl", "co")
    n_pl = n_dp // 2
    count = n_dp * n_v
    group, width = hidden.shape
    weight = head_weight[0]
    square = (n_v, n_pl, group, width)

    own = exchange(copies(hidden, n_v * n_pl), ("vk", "vs", "pl"))
    sends, t_rows = split_teacher(teacher_logits[0], n_dp)
    sends, own = lax.optimization_barrier((sends, own))
    other = lax.ppermute(own, "co", [(0, 1), (1, 0)])
    teacher = exchange(sends, ("pl", "co", "vs"))

    s_stats, lt, every_row, message = student_logits(
        own.reshape(square), other.reshape(square), t_rows, weight, count
    )
    stats_all = exchange(message, everyone)
    products, t_stats, shares = local_products(weight, teacher, lt, s_stats)
    partial_value, mass = combine(stats_all, s_stats, t_stats, products, n_v)
    pieces = exchange(partial_value.reshape(count, group, width), everyone)
    head_grad = head_gradient(shares, mass, every_row)
    hidden_grad = jnp.sum(pieces.astype(F32), axis=0).astype(BF16)
    return hidden_grad, head_grad[None]


def solution(mesh):
    n_dp, n_v = mesh.shape["dp"], mesh.shape["vocab"]
    split = Mesh(mesh.devices.reshape(n_dp // 2, 2, n_v // 2, 2), ("pl", "co", "vk", "vs"))
    dp, vocab = ("pl", "co"), ("vk", "vs")
    return jax.shard_map(
        functools.partial(shards, n_dp, n_v),
        mesh=split,
        in_specs=(P(dp, vocab), P(vocab, dp, None), P(vocab, dp, None)),
        out_specs=(P(dp, vocab), P(vocab, dp, None)),
        check_vma=False,
    )
```

profile of v0, /device:TPU:0, one launch (start us, length us, event | category | flops | bytes accessed | tf_op | source)
XLA Modules:
  0.0 79.6 jit_solution(9146812610621147353)
XLA Ops:
  0.6 1.5 %shard_map.51 = bf16[16,8,896]{2,1,0:T(8,128)(2,1)} custom-call(bf16[8,896]{1,0:T(8,128)(2,1)} %h_ref.1), custom_call_target="tpu_custom_call" | custom-call | tf_op jit(solution)/shard_map/pallas_call | solution.py:207
  2.2 8.3 %all-to-all-start = ((bf16[16,8,896]{2,1,0:T(8,128)(2,1)}), bf16[16,8,896]{2,1,0:T(8,128)(2,1)S(1)}, u32[]{:S(2)}, u32[]{:S(2)}) async-start(bf16[16,8,896]{2,1,0:T(8,128)(2,1)} %shard_map.51), calls=%async_computation | async-start | bytes 458752 | tf_op jit(solution)/shard_map/all_to_all | solution.py:438
  10.5 3.1 %shard_map.50 = (bf16[16,4,4752]{2,1,0:T(4,128)(2,1)}, f32[2,128]{1,0:T(2,128)}) custom-call(bf16[4,76032]{1,0:T(4,128)(2,1)} %bitcast.11), custom_call_target="tpu_custom_call" | custom-call | tf_op jit(solution)/shard_map/pallas_call | solution.py:249
  13.6 6.1 %all-to-all-done = bf16[16,8,896]{2,1,0:T(8,128)(2,1)S(1)} async-done(((bf16[16,8,896]{2,1,0:T(8,128)(2,1)}), bf16[16,8,896]{2,1,0:T(8,128)(2,1)S(1)}, u32[]{:S(2)}, u32[]{:S(2)}) %all-to-all-start) | async-done | bytes 229408 | tf_op jit(solution)/shard_map/all_to_all | solution.py:438
  19.7 3.6 %all-to-all-start.2 = ((bf16[16,4,4752]{2,1,0:T(4,128)(2,1)}), bf16[16,4,4752]{2,1,0:T(4,128)(2,1)S(1)}, u32[]{:S(2)}, u32[]{:S(2)}) async-start(bf16[16,4,4752]{2,1,0:T(4,128)(2,1)} %get-tuple-element.20), calls=%async_computation.2 | async-start | bytes 1245184 | tf_op jit(solution)/shard_map/all_to_all | solution.py:438
  23.3 0.3 collective-permute-start
  23.6 1.3 %collective-permute-done = bf16[16,8,896]{2,1,0:T(8,128)(2,1)S(1)} collective-permute-done((bf16[16,8,896]{2,1,0:T(8,128)(2,1)S(1)}, bf16[16,8,896]{2,1,0:T(8,128)(2,1)S(1)}, u32[]{:S(2)}, u32[]{:S(2)}) %collective-permute-start) | collective-permute-done | bytes 229408 | tf_op jit(solution)/shard_map/ppermute | solution.py:452
  24.9 15.0 %shard_map.52 = (f32[64,2]{1,0:T(8,128)S(1)}, f32[64,4752]{1,0:T(8,128)}, bf16[64,3584]{1,0:T(8,128)(2,1)}, f32[32,8,128]{2,1,0:T(8,128)}) custom-call(bf16[4,4,8,896]{3,2,1,0:T(8,128)(2,1)S(1)} %bitcast.6, bf16[4,4,8,896]{3,2,1,0:T(8,128)(2,1)S(1)} %bitcast.7, f32[2,128]{1,0:T(2,128)} %get-tuple-element.17.t_stats_ref, bf16[4752,3584]{1,0:T(8,128)(2,1)} %bitcast.8), custom_call_target="tpu_custom_call" | custom-call | flops 8719958016 | bytes 34062336 | tf_op jit(solution)/shard_map/pallas_call | solution.py:165
  39.9 0.0 all-to-all-done.2.t_ref
  39.9 4.1 %all-to-all-start.1 = ((f32[32,8,128]{2,1,0:T(8,128)}), f32[32,8,128]{2,1,0:T(8,128)S(1)}, u32[]{:S(2)}, u32[]{:S(2)}) async-start(f32[32,8,128]{2,1,0:T(8,128)} %get-tuple-element.18), calls=%async_computation.1 | async-start | bytes 262144 | tf_op jit(solution)/shard_map/all_to_all | solution.py:438
  44.0 13.5 %shard_map.53 = (f32[128,3584]{1,0:T(8,128)S(1)}, f32[64,2]{1,0:T(8,128)S(1)}, f32[4752,128]{1,0:T(8,128)}) custom-call(bf16[16,4,4752]{2,1,0:T(4,128)(2,1)S(1)} %all-to-all-done.2.t_ref, f32[64,4752]{1,0:T(8,128)} %get-tuple-element.21.lt_in, f32[64,2]{1,0:T(8,128)S(1)} %get-tuple-element.19.stats_ref.s_ref, bf16[4752,3584]{1,0:T(8,128)(2,1)} %bitcast.9), custom_call_target="tpu_custom_call" | custom-call | flops 8719958016 | bytes 34062336 | tf_op jit(solution)/shard_map/pallas_call | solution.py:305
  57.6 0.0 all-to-all-done.1.all_ref
  57.6 1.2 %shard_map.54 = (bf16[4,64,896]{2,1,0:T(8,128)(2,1)}, f32[1,128]{1,0:T(1,128)S(1)}) custom-call(f32[32,8,128]{2,1,0:T(8,128)S(1)} %all-to-all-done.1.all_ref, f32[64,2]{1,0:T(8,128)S(1)} %get-tuple-element.19.stats_ref.s_ref, f32[64,2]{1,0:T(8,128)S(1)} %get-tuple-element.22.t_ref, f32[128,3584]{1,0:T(8,128)S(1)} %get-tuple-element.23.u_ref), custom_call_target="tpu_custom_call" | custom-call | tf_op jit(solution)/shard_map/pallas_call | solution.py:351
  58.7 5.8 %all-to-all-start.3 = ((bf16[32,8,896]{2,1,0:T(8,128)(2,1)}), bf16[32,8,896]{2,1,0:T(8,128)(2,1)S(1)}, u32[]{:S(2)}, u32[]{:S(2)}) async-start(bf16[32,8,896]{2,1,0:T(8,128)(2,1)} %bitcast.12), calls=%async_computation.3 | async-start | bytes 917504 | tf_op jit(solution)/shard_map/all_to_all | solution.py:438
  64.6 13.4 %shard_map.55 = bf16[4752,3584]{1,0:T(8,128)(2,1)} custom-call(f32[4752,128]{1,0:T(8,128)} %get-tuple-element.25.both_ref, f32[1,128]{1,0:T(1,128)S(1)} %get-tuple-element.26.mass_ref, bf16[64,3584]{1,0:T(8,128)(2,1)} %get-tuple-element.27.hidden_ref), custom_call_target="tpu_custom_call" | custom-call | flops 8719958016 | bytes 34062336 | tf_op jit(solution)/shard_map/pallas_call | solution.py:418
  78.0 0.9 %all-to-all-done.3 = bf16[32,8,896]{2,1,0:T(8,128)(2,1)S(1)} async-done(((bf16[32,8,896]{2,1,0:T(8,128)(2,1)}), bf16[32,8,896]{2,1,0:T(8,128)(2,1)S(1)}, u32[]{:S(2)}, u32[]{:S(2)}) %all-to-all-start.3) | async-done | bytes 458784 | tf_op jit(solution)/shard_map/all_to_all | solution.py:438
  78.9 0.7 reduce_sum.12
Async XLA Ops:
  2.2 17.6 %all-to-all-start = ((bf16[16,8,896]{2,1,0:T(8,128)(2,1)}), bf16[16,8,896]{2,1,0:T(8,128)(2,1)S(1)}, u32[]{:S(2)}, u32[]{:S(2)}) async-start(bf16[16,8,896]{2,1,0:T(8,128)(2,1)} %shard_map.51), calls=%async_computation | async-start | bytes 458752 | tf_op jit(solution)/shard_map/all_to_all | solution.py:438
  19.7 20.2 %all-to-all-start.2 = ((bf16[16,4,4752]{2,1,0:T(4,128)(2,1)}), bf16[16,4,4752]{2,1,0:T(4,128)(2,1)S(1)}, u32[]{:S(2)}, u32[]{:S(2)}) async-start(bf16[16,4,4752]{2,1,0:T(4,128)(2,1)} %get-tuple-element.20), calls=%async_computation.2 | async-start | bytes 1245184 | tf_op jit(solution)/shard_map/all_to_all | solution.py:438
  23.3 1.6 %collective-permute-start = (bf16[16,8,896]{2,1,0:T(8,128)(2,1)S(1)}, bf16[16,8,896]{2,1,0:T(8,128)(2,1)S(1)}, u32[]{:S(2)}, u32[]{:S(2)}) collective-permute-start(bf16[16,8,896]{2,1,0:T(8,128)(2,1)S(1)} %all-to-all-done), channel_id=1, source_target_pairs={{0,4},{4,0},{1,5},{5,1},{2,6},{6,2},{3,7},{7,3},{8,12},{12,8},{9,1... | collective-permute-start | bytes 688136 | tf_op jit(solution)/shard_map/ppermute | solution.py:452
  39.9 17.6 %all-to-all-start.1 = ((f32[32,8,128]{2,1,0:T(8,128)}), f32[32,8,128]{2,1,0:T(8,128)S(1)}, u32[]{:S(2)}, u32[]{:S(2)}) async-start(f32[32,8,128]{2,1,0:T(8,128)} %get-tuple-element.18), calls=%async_computation.1 | async-start | bytes 262144 | tf_op jit(solution)/shard_map/all_to_all | solution.py:438
  58.7 20.2 %all-to-all-start.3 = ((bf16[32,8,896]{2,1,0:T(8,128)(2,1)}), bf16[32,8,896]{2,1,0:T(8,128)(2,1)S(1)}, u32[]{:S(2)}, u32[]{:S(2)}) async-start(bf16[32,8,896]{2,1,0:T(8,128)(2,1)} %bitcast.12), calls=%async_computation.3 | async-start | bytes 917504 | tf_op jit(solution)/shard_map/all_to_all | solution.py:438
where the time goes:
time: 80.2 us; the launch traced here: 79.6 us
  Pallas kernels  47.9 us (60%)
  starting transfers between devices  22.1 us (28%)
  waiting for transfers between devices  8.28 us (10%)
    all_to_all x4, starting transfers between devices, exchange(): return lax.all_to_all(parts, axes, split_axis=0, concat_axis=0, tiled=True)  21.8 us
    pallas_call x1, Pallas kernels, student_logits(): pl.pallas_call(logits_kernel, in_specs=[*in_vmem(2), anywhere, anywhere],...  15 us
    pallas_call x1, Pallas kernels, local_products(): pl.pallas_call(products_kernel, in_specs=[*in_vmem(1), anywhere, *in_vmem...  13.5 us
    pallas_call x1, Pallas kernels, head_gradient(): pl.pallas_call(functools.partial(head_kernel, tile), in_specs=[anywhere,...  13.4 us
    all_to_all x4, waiting for transfers between devices, exchange(): return lax.all_to_all(parts, axes, split_axis=0, concat_axis=0, tiled=True)  7.02 us
    pallas_call x1, Pallas kernels, split_teacher(): pl.pallas_call(split_kernel, in_specs=[pl.BlockSpec(memory_space=pl.ANY)]...  3.14 us
  transfers between devices with their start and end apart: 5, of which 3 were waited for; matrix products, arithmetic and copies ran while one was open for 0% of the time, Pallas kernels for 57%

commit v1 on v0

--- a/solution.py
+++ b/solution.py
@@ -48,7 +48,7 @@
     return [pl.BlockSpec(memory_space=pltpu.VMEM)] * count
 
 
-def stream(w_ref, buffer, sems, first, tile, ahead, compute, between):
+def stream(w_ref, buffer, sems, first, tile, ahead, compute, between, beside=None):
     rows = w_ref.shape[0]
     if rows < first + tile:
         first = 0
@@ -73,6 +73,8 @@
     if first:
         copy(begin, sems.at[steps + 1]).wait()
         compute(begin, steps + 1)
+        if beside is not None:
+            beside()
 
     def body(step, carry):
         @pl.when(step + ahead < steps)
@@ -270,31 +272,46 @@
     tokens = stats_ref.shape[0]
     load.start()
 
+    rows = w_ref.shape[0]
+    early = 512 if rows >= 512 + PRODUCT_TILE else rows
+
+    def shares_of(here):
+        values = jnp.concatenate(
+            [t_ref[j][:, here].astype(F32) for j in range(t_ref.shape[0])], axis=0
+        )
+        teach = jnp.exp(values - t_stats_ref[:, 0:1]) * (1.0 / t_stats_ref[:, 1:2])
+        share = jnp.exp(lt_ref[:, here] - stats_ref[:, 0:1]) * (1.0 / stats_ref[:, 1:2])
+        packed[:tokens, here] = (share - teach).astype(BF16)
+        packed[tokens:, here] = teach.astype(BF16)
+        both[here, :] = jnp.concatenate([share, teach], axis=0).T
+
     def prepare():
         values = teacher_values(t_ref)
         top = jnp.max(values, axis=1, keepdims=True)
-        weights = jnp.exp(values - top)
-        total = jnp.sum(weights, axis=1, keepdims=True)
+        total = jnp.sum(jnp.exp(values - top), axis=1, keepdims=True)
         t_stats_ref[...] = jnp.concatenate([top, total], axis=1)
-        teach = weights * (1.0 / total)
         load.wait()
-        share = jnp.exp(lt_ref[...] - stats_ref[:, 0:1]) * (1.0 / stats_ref[:, 1:2])
-        both[...] = jnp.concatenate([share, teach], axis=0).T
-        packed[:tokens, :] = (share - teach).astype(BF16)
-        packed[tokens:, :] = teach.astype(BF16)
+        shares_of(slice(0, early))
+        if early == rows:
+            u_ref[...] = jnp.zeros_like(u_ref)
+            keep.start()
+
+    def prepare_rest():
+        shares_of(slice(early, rows))
         keep.start()
-        u_ref[...] = jnp.zeros_like(u_ref)
 
     def compute(here, index):
         width = u_ref.shape[1]
         block = column_tile(width, 512)
         for k in range(0, width, block):
             cols = slice(k, k + block)
-            u_ref[:, cols] += jnp.dot(
-                packed[:, here], buffer[here, cols], preferred_element_type=F32
-            )
-
-    stream(w_ref, buffer, sems, 512, PRODUCT_TILE, 2, compute, prepare)
+            value = jnp.dot(packed[:, here], buffer[here, cols], preferred_element_type=F32)
+            if early < rows and isinstance(here, slice) and here.start == 0:
+                u_ref[:, cols] = value
+            else:
+                u_ref[:, cols] += value
+
+    stream(w_ref, buffer, sems, 512, PRODUCT_TILE, 2, compute, prepare, prepare_rest)
     keep.wait()
 
 

time: 80.2 us -> 79.9 us (level)
  no operation moved by 1% of the time
where the time goes in v1:
time: 79.9 us; the launch traced here: 79.4 us
  Pallas kernels  47.6 us (60%)
  starting transfers between devices  22.1 us (28%)
  waiting for transfers between devices  8.28 us (10%)
    all_to_all x4, starting transfers between devices, exchange(): return lax.all_to_all(parts, axes, split_axis=0, concat_axis=0, tiled=True)  21.8 us
    pallas_call x1, Pallas kernels, student_logits(): pl.pallas_call(logits_kernel, in_specs=[*in_vmem(2), anywhere, anywhere],...  15 us
    pallas_call x1, Pallas kernels, head_gradient(): pl.pallas_call(functools.partial(head_kernel, tile), in_specs=[anywhere,...  13.4 us
    pallas_call x1, Pallas kernels, local_products(): pl.pallas_call(products_kernel, in_specs=[*in_vmem(1), anywhere, *in_vmem...  13.3 us
    all_to_all x4, waiting for transfers between devices, exchange(): return lax.all_to_all(parts, axes, split_axis=0, concat_axis=0, tiled=True)  7.02 us
    pallas_call x1, Pallas kernels, split_teacher(): pl.pallas_call(split_kernel, in_specs=[pl.BlockSpec(memory_space=pl.ANY)]...  3.14 us
  transfers between devices with their start and end apart: 5, of which 3 were waited for; matrix products, arithmetic and copies ran while one was open for 0% of the time, Pallas kernels for 57%

profile of v1, /device:TPU:0, one launch (start us, length us, event | category | flops | bytes accessed | tf_op | source)
XLA Modules:
  0.0 79.4 jit_solution(7902381526412480324)
XLA Ops:
  0.6 1.5 %shard_map.51 = bf16[16,8,896]{2,1,0:T(8,128)(2,1)} custom-call(bf16[8,896]{1,0:T(8,128)(2,1)} %h_ref.1), custom_call_target="tpu_custom_call" | custom-call | tf_op jit(solution)/shard_map/pallas_call | solution.py:209
  2.2 8.3 %all-to-all-start = ((bf16[16,8,896]{2,1,0:T(8,128)(2,1)}), bf16[16,8,896]{2,1,0:T(8,128)(2,1)S(1)}, u32[]{:S(2)}, u32[]{:S(2)}) async-start(bf16[16,8,896]{2,1,0:T(8,128)(2,1)} %shard_map.51), calls=%async_computation | async-start | bytes 458752 | tf_op jit(solution)/shard_map/all_to_all | solution.py:455
  10.5 3.1 %shard_map.50 = (bf16[16,4,4752]{2,1,0:T(4,128)(2,1)}, f32[2,128]{1,0:T(2,128)}) custom-call(bf16[4,76032]{1,0:T(4,128)(2,1)} %bitcast.11), custom_call_target="tpu_custom_call" | custom-call | tf_op jit(solution)/shard_map/pallas_call | solution.py:251
  13.6 6.1 %all-to-all-done = bf16[16,8,896]{2,1,0:T(8,128)(2,1)S(1)} async-done(((bf16[16,8,896]{2,1,0:T(8,128)(2,1)}), bf16[16,8,896]{2,1,0:T(8,128)(2,1)S(1)}, u32[]{:S(2)}, u32[]{:S(2)}) %all-to-all-start) | async-done | bytes 229408 | tf_op jit(solution)/shard_map/all_to_all | solution.py:455
  19.7 3.6 %all-to-all-start.2 = ((bf16[16,4,4752]{2,1,0:T(4,128)(2,1)}), bf16[16,4,4752]{2,1,0:T(4,128)(2,1)S(1)}, u32[]{:S(2)}, u32[]{:S(2)}) async-start(bf16[16,4,4752]{2,1,0:T(4,128)(2,1)} %get-tuple-element.20), calls=%async_computation.2 | async-start | bytes 1245184 | tf_op jit(solution)/shard_map/all_to_all | solution.py:455
  23.3 0.3 collective-permute-start
  23.6 1.3 %collective-permute-done = bf16[16,8,896]{2,1,0:T(8,128)(2,1)S(1)} collective-permute-done((bf16[16,8,896]{2,1,0:T(8,128)(2,1)S(1)}, bf16[16,8,896]{2,1,0:T(8,128)(2,1)S(1)}, u32[]{:S(2)}, u32[]{:S(2)}) %collective-permute-start) | collective-permute-done | bytes 229408 | tf_op jit(solution)/shard_map/ppermute | solution.py:469
  24.9 15.0 %shard_map.52 = (f32[64,2]{1,0:T(8,128)S(1)}, f32[64,4752]{1,0:T(8,128)}, bf16[64,3584]{1,0:T(8,128)(2,1)}, f32[32,8,128]{2,1,0:T(8,128)}) custom-call(bf16[4,4,8,896]{3,2,1,0:T(8,128)(2,1)S(1)} %bitcast.6, bf16[4,4,8,896]{3,2,1,0:T(8,128)(2,1)S(1)} %bitcast.7, f32[2,128]{1,0:T(2,128)} %get-tuple-element.17.t_stats_ref, bf16[4752,3584]{1,0:T(8,128)(2,1)} %bitcast.8), custom_call_target="tpu_custom_call" | custom-call | flops 8719958016 | bytes 34062336 | tf_op jit(solution)/shard_map/pallas_call | solution.py:167
  39.9 0.0 all-to-all-done.2.t_ref
  39.9 4.1 %all-to-all-start.1 = ((f32[32,8,128]{2,1,0:T(8,128)}), f32[32,8,128]{2,1,0:T(8,128)S(1)}, u32[]{:S(2)}, u32[]{:S(2)}) async-start(f32[32,8,128]{2,1,0:T(8,128)} %get-tuple-element.18), calls=%async_computation.1 | async-start | bytes 262144 | tf_op jit(solution)/shard_map/all_to_all | solution.py:455
  44.0 13.3 %shard_map.53 = (f32[128,3584]{1,0:T(8,128)S(1)}, f32[64,2]{1,0:T(8,128)S(1)}, f32[4752,128]{1,0:T(8,128)}) custom-call(bf16[16,4,4752]{2,1,0:T(4,128)(2,1)S(1)} %all-to-all-done.2.t_ref, f32[64,4752]{1,0:T(8,128)} %get-tuple-element.21.lt_in, f32[64,2]{1,0:T(8,128)S(1)} %get-tuple-element.19.stats_ref.s_ref, bf16[4752,3584]{1,0:T(8,128)(2,1)} %bitcast.9), custom_call_target="tpu_custom_call" | custom-call | flops 8719958016 | bytes 34062336 | tf_op jit(solution)/shard_map/pallas_call | solution.py:322
  57.3 0.0 all-to-all-done.1.all_ref
  57.3 1.2 %shard_map.54 = (bf16[4,64,896]{2,1,0:T(8,128)(2,1)}, f32[1,128]{1,0:T(1,128)S(1)}) custom-call(f32[32,8,128]{2,1,0:T(8,128)S(1)} %all-to-all-done.1.all_ref, f32[64,2]{1,0:T(8,128)S(1)} %get-tuple-element.19.stats_ref.s_ref, f32[64,2]{1,0:T(8,128)S(1)} %get-tuple-element.22.t_ref, f32[128,3584]{1,0:T(8,128)S(1)} %get-tuple-element.23.u_ref), custom_call_target="tpu_custom_call" | custom-call | tf_op jit(solution)/shard_map/pallas_call | solution.py:368
  58.5 5.8 %all-to-all-start.3 = ((bf16[32,8,896]{2,1,0:T(8,128)(2,1)}), bf16[32,8,896]{2,1,0:T(8,128)(2,1)S(1)}, u32[]{:S(2)}, u32[]{:S(2)}) async-start(bf16[32,8,896]{2,1,0:T(8,128)(2,1)} %bitcast.12), calls=%async_computation.3 | async-start | bytes 917504 | tf_op jit(solution)/shard_map/all_to_all | solution.py:455
  64.4 13.4 %shard_map.55 = bf16[4752,3584]{1,0:T(8,128)(2,1)} custom-call(f32[4752,128]{1,0:T(8,128)} %get-tuple-element.25.both_ref, f32[1,128]{1,0:T(1,128)S(1)} %get-tuple-element.26.mass_ref, bf16[64,3584]{1,0:T(8,128)(2,1)} %get-tuple-element.27.hidden_ref), custom_call_target="tpu_custom_call" | custom-call | flops 8719958016 | bytes 34062336 | tf_op jit(solution)/shard_map/pallas_call | solution.py:435
  77.8 0.9 %all-to-all-done.3 = bf16[32,8,896]{2,1,0:T(8,128)(2,1)S(1)} async-done(((bf16[32,8,896]{2,1,0:T(8,128)(2,1)}), bf16[32,8,896]{2,1,0:T(8,128)(2,1)S(1)}, u32[]{:S(2)}, u32[]{:S(2)}) %all-to-all-start.3) | async-done | bytes 458784 | tf_op jit(solution)/shard_map/all_to_all | solution.py:455
  78.7 0.7 reduce_sum.12
Async XLA Ops:
  2.2 17.6 %all-to-all-start = ((bf16[16,8,896]{2,1,0:T(8,128)(2,1)}), bf16[16,8,896]{2,1,0:T(8,128)(2,1)S(1)}, u32[]{:S(2)}, u32[]{:S(2)}) async-start(bf16[16,8,896]{2,1,0:T(8,128)(2,1)} %shard_map.51), calls=%async_computation | async-start | bytes 458752 | tf_op jit(solution)/shard_map/all_to_all | solution.py:455
  19.7 20.2 %all-to-all-start.2 = ((bf16[16,4,4752]{2,1,0:T(4,128)(2,1)}), bf16[16,4,4752]{2,1,0:T(4,128)(2,1)S(1)}, u32[]{:S(2)}, u32[]{:S(2)}) async-start(bf16[16,4,4752]{2,1,0:T(4,128)(2,1)} %get-tuple-element.20), calls=%async_computation.2 | async-start | bytes 1245184 | tf_op jit(solution)/shard_map/all_to_all | solution.py:455
  23.3 1.6 %collective-permute-start = (bf16[16,8,896]{2,1,0:T(8,128)(2,1)S(1)}, bf16[16,8,896]{2,1,0:T(8,128)(2,1)S(1)}, u32[]{:S(2)}, u32[]{:S(2)}) collective-permute-start(bf16[16,8,896]{2,1,0:T(8,128)(2,1)S(1)} %all-to-all-done), channel_id=1, source_target_pairs={{0,4},{4,0},{1,5},{5,1},{2,6},{6,2},{3,7},{7,3},{8,12},{12,8},{9,1... | collective-permute-start | bytes 688136 | tf_op jit(solution)/shard_map/ppermute | solution.py:469
  39.9 17.4 %all-to-all-start.1 = ((f32[32,8,128]{2,1,0:T(8,128)}), f32[32,8,128]{2,1,0:T(8,128)S(1)}, u32[]{:S(2)}, u32[]{:S(2)}) async-start(f32[32,8,128]{2,1,0:T(8,128)} %get-tuple-element.18), calls=%async_computation.1 | async-start | bytes 262144 | tf_op jit(solution)/shard_map/all_to_all | solution.py:455
  58.5 20.2 %all-to-all-start.3 = ((bf16[32,8,896]{2,1,0:T(8,128)(2,1)}), bf16[32,8,896]{2,1,0:T(8,128)(2,1)S(1)}, u32[]{:S(2)}, u32[]{:S(2)}) async-start(bf16[32,8,896]{2,1,0:T(8,128)(2,1)} %bitcast.12), calls=%async_computation.3 | async-start | bytes 917504 | tf_op jit(solution)/shard_map/all_to_all | solution.py:455

commit v2 on v1

--- a/solution.py
+++ b/solution.py
@@ -115,8 +115,8 @@
 
 
 def logits_kernel(own_ref, other_ref, t_stats_ref, w_ref, *refs):
-    stats_ref, lt_out, out_ref, message_ref, *scratch = refs
-    lt_ref, hidden, buffer, staged, t_stats, sems, lt_sems, out_sems = scratch
+    stats_ref, lt_out, out_ref, message_out, *scratch = refs
+    lt_ref, hidden, buffer, staged, t_stats, message_ref, sems, lt_sems, out_sems = scratch
     keep = pltpu.make_async_copy(hidden, out_ref, out_sems.at[0])
     load = pltpu.make_async_copy(t_stats_ref, t_stats, out_sems.at[1])
     load.start()
@@ -154,9 +154,12 @@
     message = jnp.concatenate([lines, t_stats[...], jnp.zeros((4, lanes), F32)], axis=0)
     for k in range(message_ref.shape[0]):
         message_ref[k] = message
+    send_message = pltpu.make_async_copy(message_ref, message_out, out_sems.at[2])
+    send_message.start()
     keep.wait()
     for index, here in chunks:
         send(here, index).wait()
+    send_message.wait()
 
 
 def student_logits(own, other, t_stats, weight, count):
@@ -167,7 +170,7 @@
     return pl.pallas_call(
         logits_kernel,
         in_specs=[*in_vmem(2), anywhere, anywhere],
-        out_specs=[*in_vmem(1), anywhere, anywhere, *in_vmem(1)],
+        out_specs=[*in_vmem(1), anywhere, anywhere, anywhere],
         out_shape=[
             jax.ShapeDtypeStruct((tokens, 2), F32),
             pltpu.HBM((tokens, rows), F32),
@@ -180,9 +183,10 @@
             pltpu.VMEM((rows, width), BF16),
             pltpu.VMEM((2, *own.shape), F32),
             pltpu.VMEM(t_stats.shape, F32),
+            pltpu.VMEM((count, 8, t_stats.shape[1]), F32),
             pltpu.SemaphoreType.DMA((rows // LOGIT_TILE + 2,)),
             pltpu.SemaphoreType.DMA((rows // LOGIT_TILE + 2,)),
-            pltpu.SemaphoreType.DMA((2,)),
+            pltpu.SemaphoreType.DMA((3,)),
         ],
         compiler_params=params(46 * MIB),
         cost_estimate=pl.CostEstimate(
@@ -343,7 +347,7 @@
     )(teacher, pltpu.with_memory_space_constraint(lt, pltpu.HBM), stats, weight)
 
 
-def combine_kernel(all_ref, s_ref, t_ref, u_ref, hp_ref, mass_ref):
+def combine_kernel(all_ref, s_ref, t_ref, u_ref, hp_out, mass_ref, hp_ref, sems):
     tokens = s_ref.shape[0]
 
     def mass(k, mine_ref):
@@ -357,9 +361,14 @@
     scale_x = GRAD_SCALE * student
     scale_t = GRAD_SCALE * (student - teacher)
     width = hp_ref.shape[2]
+    sends = []
     for v in range(hp_ref.shape[0]):
         cols = slice(v * width, (v + 1) * width)
         hp_ref[v] = (u_ref[:tokens, cols] * scale_x + u_ref[tokens:, cols] * scale_t).astype(BF16)
+        sends.append(pltpu.make_async_copy(hp_ref.at[v], hp_out.at[v], sems.at[v]))
+        sends[-1].start()
+    for send in sends:
+        send.wait()
 
 
 def combine(stats_all, s_stats, t_stats, products, n_v):
@@ -368,10 +377,14 @@
     return pl.pallas_call(
         combine_kernel,
         in_specs=in_vmem(4),
-        out_specs=in_vmem(2),
+        out_specs=[pl.BlockSpec(memory_space=pl.ANY), *in_vmem(1)],
         out_shape=[
             pltpu.HBM((n_v, tokens, width), BF16),
             jax.ShapeDtypeStruct((1, 2 * tokens), F32),
+        ],
+        scratch_shapes=[
+            pltpu.VMEM((n_v, tokens, width), BF16),
+            pltpu.SemaphoreType.DMA((n_v,)),
         ],
         compiler_params=params(12 * MIB),
     )(stats_all, s_stats, t_stats, products)

time: 79.9 us -> 79.7 us (level)
  transfers between devices with their start and end apart: 5 -> 5, of which waited for: 3 -> 3; matrix products, arithmetic and copies ran while one was open for 0% -> 0% of each run, Pallas kernels for 57% -> 56%
where the time goes in v2:
time: 79.7 us; the launch traced here: 79.1 us
  Pallas kernels  47.3 us (59%)
  starting transfers between devices  22.1 us (28%)
  waiting for transfers between devices  8.27 us (10%)
    all_to_all x4, starting transfers between devices, exchange(): return lax.all_to_all(parts, axes, split_axis=0, concat_axis=0, tiled=True)  21.8 us
    pallas_call x1, Pallas kernels, student_logits(): pl.pallas_call(logits_kernel, in_specs=[*in_vmem(2), anywhere, anywhere],...  14.7 us
    pallas_call x1, Pallas kernels, head_gradient(): pl.pallas_call(functools.partial(head_kernel, tile), in_specs=[anywhere,...  13.5 us
    pallas_call x1, Pallas kernels, local_products(): pl.pallas_call(products_kernel, in_specs=[*in_vmem(1), anywhere, *in_vmem...  13.3 us
    all_to_all x4, waiting for transfers between devices, exchange(): return lax.all_to_all(parts, axes, split_axis=0, concat_axis=0, tiled=True)  7.02 us
    pallas_call x1, Pallas kernels, split_teacher(): pl.pallas_call(split_kernel, in_specs=[pl.BlockSpec(memory_space=pl.ANY)]...  3.14 us
  transfers between devices with their start and end apart: 5, of which 3 were waited for; matrix products, arithmetic and copies ran while one was open for 0% of the time, Pallas kernels for 56%

profile of v2, /device:TPU:0, one launch (start us, length us, event | category | flops | bytes accessed | tf_op | source)
XLA Modules:
  0.0 79.1 jit_solution(13323326701012570965)
XLA Ops:
  0.6 1.5 %shard_map.51 = bf16[16,8,896]{2,1,0:T(8,128)(2,1)} custom-call(bf16[8,896]{1,0:T(8,128)(2,1)} %h_ref.1), custom_call_target="tpu_custom_call" | custom-call | tf_op jit(solution)/shard_map/pallas_call | solution.py:213
  2.2 8.3 %all-to-all-start = ((bf16[16,8,896]{2,1,0:T(8,128)(2,1)}), bf16[16,8,896]{2,1,0:T(8,128)(2,1)S(1)}, u32[]{:S(2)}, u32[]{:S(2)}) async-start(bf16[16,8,896]{2,1,0:T(8,128)(2,1)} %shard_map.51), calls=%async_computation | async-start | bytes 458752 | tf_op jit(solution)/shard_map/all_to_all | solution.py:468
  10.5 3.1 %shard_map.50 = (bf16[16,4,4752]{2,1,0:T(4,128)(2,1)}, f32[2,128]{1,0:T(2,128)}) custom-call(bf16[4,76032]{1,0:T(4,128)(2,1)} %bitcast.11), custom_call_target="tpu_custom_call" | custom-call | tf_op jit(solution)/shard_map/pallas_call | solution.py:255
  13.6 6.1 %all-to-all-done = bf16[16,8,896]{2,1,0:T(8,128)(2,1)S(1)} async-done(((bf16[16,8,896]{2,1,0:T(8,128)(2,1)}), bf16[16,8,896]{2,1,0:T(8,128)(2,1)S(1)}, u32[]{:S(2)}, u32[]{:S(2)}) %all-to-all-start) | async-done | bytes 229408 | tf_op jit(solution)/shard_map/all_to_all | solution.py:468
  19.7 3.6 %all-to-all-start.2 = ((bf16[16,4,4752]{2,1,0:T(4,128)(2,1)}), bf16[16,4,4752]{2,1,0:T(4,128)(2,1)S(1)}, u32[]{:S(2)}, u32[]{:S(2)}) async-start(bf16[16,4,4752]{2,1,0:T(4,128)(2,1)} %get-tuple-element.20), calls=%async_computation.2 | async-start | bytes 1245184 | tf_op jit(solution)/shard_map/all_to_all | solution.py:468
  23.3 0.3 collective-permute-start
  23.6 1.3 %collective-permute-done = bf16[16,8,896]{2,1,0:T(8,128)(2,1)S(1)} collective-permute-done((bf16[16,8,896]{2,1,0:T(8,128)(2,1)S(1)}, bf16[16,8,896]{2,1,0:T(8,128)(2,1)S(1)}, u32[]{:S(2)}, u32[]{:S(2)}) %collective-permute-start) | collective-permute-done | bytes 229408 | tf_op jit(solution)/shard_map/ppermute | solution.py:482
  24.9 14.7 %shard_map.52 = (f32[64,2]{1,0:T(8,128)S(1)}, f32[64,4752]{1,0:T(8,128)}, bf16[64,3584]{1,0:T(8,128)(2,1)}, f32[32,8,128]{2,1,0:T(8,128)}) custom-call(bf16[4,4,8,896]{3,2,1,0:T(8,128)(2,1)S(1)} %bitcast.6, bf16[4,4,8,896]{3,2,1,0:T(8,128)(2,1)S(1)} %bitcast.7, f32[2,128]{1,0:T(2,128)} %get-tuple-element.17.t_stats_ref, bf16[4752,3584]{1,0:T(8,128)(2,1)} %bitcast.8), custom_call_target="tpu_custom_call" | custom-call | flops 8719958016 | bytes 34062336 | tf_op jit(solution)/shard_map/pallas_call | solution.py:170
  39.6 0.0 all-to-all-done.2.t_ref
  39.6 4.1 %all-to-all-start.1 = ((f32[32,8,128]{2,1,0:T(8,128)}), f32[32,8,128]{2,1,0:T(8,128)S(1)}, u32[]{:S(2)}, u32[]{:S(2)}) async-start(f32[32,8,128]{2,1,0:T(8,128)} %get-tuple-element.18), calls=%async_computation.1 | async-start | bytes 262144 | tf_op jit(solution)/shard_map/all_to_all | solution.py:468
  43.7 13.3 %shard_map.53 = (f32[128,3584]{1,0:T(8,128)S(1)}, f32[64,2]{1,0:T(8,128)S(1)}, f32[4752,128]{1,0:T(8,128)}) custom-call(bf16[16,4,4752]{2,1,0:T(4,128)(2,1)S(1)} %all-to-all-done.2.t_ref, f32[64,4752]{1,0:T(8,128)} %get-tuple-element.21.lt_in, f32[64,2]{1,0:T(8,128)S(1)} %get-tuple-element.19.stats_ref.s_ref, bf16[4752,3584]{1,0:T(8,128)(2,1)} %bitcast.9), custom_call_target="tpu_custom_call" | custom-call | flops 8719958016 | bytes 34062336 | tf_op jit(solution)/shard_map/pallas_call | solution.py:326
  57.0 0.0 all-to-all-done.1.all_ref
  57.0 1.2 %shard_map.54 = (bf16[4,64,896]{2,1,0:T(8,128)(2,1)}, f32[1,128]{1,0:T(1,128)S(1)}) custom-call(f32[32,8,128]{2,1,0:T(8,128)S(1)} %all-to-all-done.1.all_ref, f32[64,2]{1,0:T(8,128)S(1)} %get-tuple-element.19.stats_ref.s_ref, f32[64,2]{1,0:T(8,128)S(1)} %get-tuple-element.22.t_ref, f32[128,3584]{1,0:T(8,128)S(1)} %get-tuple-element.23.u_ref), custom_call_target="tpu_custom_call" | custom-call | tf_op jit(solution)/shard_map/pallas_call | solution.py:377
  58.2 5.8 %all-to-all-start.3 = ((bf16[32,8,896]{2,1,0:T(8,128)(2,1)}), bf16[32,8,896]{2,1,0:T(8,128)(2,1)S(1)}, u32[]{:S(2)}, u32[]{:S(2)}) async-start(bf16[32,8,896]{2,1,0:T(8,128)(2,1)} %bitcast.12), calls=%async_computation.3 | async-start | bytes 917504 | tf_op jit(solution)/shard_map/all_to_all | solution.py:468
  64.1 13.5 %shard_map.55 = bf16[4752,3584]{1,0:T(8,128)(2,1)} custom-call(f32[4752,128]{1,0:T(8,128)} %get-tuple-element.25.both_ref, f32[1,128]{1,0:T(1,128)S(1)} %get-tuple-element.26.mass_ref, bf16[64,3584]{1,0:T(8,128)(2,1)} %get-tuple-element.27.hidden_ref), custom_call_target="tpu_custom_call" | custom-call | flops 8719958016 | bytes 34062336 | tf_op jit(solution)/shard_map/pallas_call | solution.py:448
  77.5 0.9 %all-to-all-done.3 = bf16[32,8,896]{2,1,0:T(8,128)(2,1)S(1)} async-done(((bf16[32,8,896]{2,1,0:T(8,128)(2,1)}), bf16[32,8,896]{2,1,0:T(8,128)(2,1)S(1)}, u32[]{:S(2)}, u32[]{:S(2)}) %all-to-all-start.3) | async-done | bytes 458784 | tf_op jit(solution)/shard_map/all_to_all | solution.py:468
  78.4 0.7 reduce_sum.12
Async XLA Ops:
  2.2 17.6 %all-to-all-start = ((bf16[16,8,896]{2,1,0:T(8,128)(2,1)}), bf16[16,8,896]{2,1,0:T(8,128)(2,1)S(1)}, u32[]{:S(2)}, u32[]{:S(2)}) async-start(bf16[16,8,896]{2,1,0:T(8,128)(2,1)} %shard_map.51), calls=%async_computation | async-start | bytes 458752 | tf_op jit(solution)/shard_map/all_to_all | solution.py:468
  19.7 19.9 %all-to-all-start.2 = ((bf16[16,4,4752]{2,1,0:T(4,128)(2,1)}), bf16[16,4,4752]{2,1,0:T(4,128)(2,1)S(1)}, u32[]{:S(2)}, u32[]{:S(2)}) async-start(bf16[16,4,4752]{2,1,0:T(4,128)(2,1)} %get-tuple-element.20), calls=%async_computation.2 | async-start | bytes 1245184 | tf_op jit(solution)/shard_map/all_to_all | solution.py:468
  23.3 1.6 %collective-permute-start = (bf16[16,8,896]{2,1,0:T(8,128)(2,1)S(1)}, bf16[16,8,896]{2,1,0:T(8,128)(2,1)S(1)}, u32[]{:S(2)}, u32[]{:S(2)}) collective-permute-start(bf16[16,8,896]{2,1,0:T(8,128)(2,1)S(1)} %all-to-all-done), channel_id=1, source_target_pairs={{0,4},{4,0},{1,5},{5,1},{2,6},{6,2},{3,7},{7,3},{8,12},{12,8},{9,1... | collective-permute-start | bytes 688136 | tf_op jit(solution)/shard_map/ppermute | solution.py:482
  39.6 17.4 %all-to-all-start.1 = ((f32[32,8,128]{2,1,0:T(8,128)}), f32[32,8,128]{2,1,0:T(8,128)S(1)}, u32[]{:S(2)}, u32[]{:S(2)}) async-start(f32[32,8,128]{2,1,0:T(8,128)} %get-tuple-element.18), calls=%async_computation.1 | async-start | bytes 262144 | tf_op jit(solution)/shard_map/all_to_all | solution.py:468
  58.2 20.2 %all-to-all-start.3 = ((bf16[32,8,896]{2,1,0:T(8,128)(2,1)}), bf16[32,8,896]{2,1,0:T(8,128)(2,1)S(1)}, u32[]{:S(2)}, u32[]{:S(2)}) async-start(bf16[32,8,896]{2,1,0:T(8,128)(2,1)} %bitcast.12), calls=%async_computation.3 | async-start | bytes 917504 | tf_op jit(solution)/shard_map/all_to_all | solution.py:468
